TPU v7x, 512 devices: a whole 4x8x8 slice. The times are simulated.
512 devices in a mesh: cluster: 32 (over z_hi, x, core), blk: 16 (over y, z_lo).
Axes of the slice: x: 4, y: 8, z: 8 (z_hi: 4, z_lo: 2; z = z_hi * 2 + z_lo), core: 2. Of those that a mesh axis runs over, the one named last changes fastest.
Arguments:
- coeff: bfloat16 [1024, 8, 2048], P('cluster', None, 'blk'), may hold values from -0.375 to 0.375
- intersection: int32 [32, 32], replicated, may hold values from 0 to 1023, as said below
- basis_vals: bfloat16 [131072, 256], P(('cluster', 'blk')), may hold values from -6 to 6
- coulomb: bfloat16 [131072, 7, 256], P(('cluster', 'blk')), may hold values from -0.125 to 0.125
- reach: int32 [512], P(('cluster', 'blk')), may hold values from 0 to 3, as said below
Outputs:
- exchange_out: bfloat16 [131072, 2048], P(('cluster', 'blk'))
Inputs may be any that keep to these rules, and one draw needn't show every extreme that they name: `intersection`: each row lists 32 distinct atoms; atom a is owned by cluster a // 32; at most 2 atoms of one row have the same owner, and each row c holds exactly 2 atoms owned by cluster c. `reach`: some block reaches 3 and some block reaches 0.
All inputs are finite; a program needn't handle non-finite values.
Results may differ from a plain program's by a relative error of at most 0.0059.
Values may be sent and summed in bfloat16 or wider, within the bound.
A program may use at most 64 MiB of HBM per device.

v0:
```python
import jax
import jax.numpy as jnp
from jax import lax
from jax.sharding import PartitionSpec as P


def passed_along(value, axis, steps):
    count = lax.axis_size(axis)
    pairs = [(source, (source + steps) % count) for source in range(count)]
    return lax.ppermute(value, axis, pairs)


def block_term(local_vals, source, coul_tile, within, norm_factor):
    density = (
        lax.dot_general(
            local_vals, source, (((1,), (1,)), ((), ())), preferred_element_type=jnp.float32
        )
        * norm_factor
    )
    masked_tile = jnp.where(
        within, density * coul_tile.astype(jnp.float32), jnp.float32(0.0)
    ).astype(jnp.bfloat16)
    return jnp.dot(masked_tile, source, preferred_element_type=jnp.float32)


def on_device(coeff, intersection, basis_vals, coulomb, reach):
    num_clusters = lax.axis_size("cluster")
    my_cluster = lax.axis_index("cluster")
    atom_count = coeff.shape[0]
    list_len = intersection.shape[1]
    capacity = 2 * list_len // num_clusters
    num_funcs = coeff.shape[1]
    my_columns = coeff.shape[2]
    half_stops = (coulomb.shape[1] - 1) // 2
    owners = intersection // atom_count
    same_owner = owners[:, :, None] == owners[:, None, :]
    earlier = jnp.arange(list_len)[None, :] < jnp.arange(list_len)[:, None]
    slot_rank = jnp.sum(jnp.logical_and(same_owner, earlier[None, :, :]).astype(jnp.int32), axis=2)
    matches = jnp.logical_and(
        (owners == my_cluster)[:, :, None],
        slot_rank[:, :, None] == jnp.arange(capacity)[None, None, :],
    )
    local_atom = intersection - my_cluster * atom_count
    source_rows = jnp.sum(jnp.where(matches, local_atom[:, :, None], 0), axis=1)
    filled = jnp.any(matches, axis=1)
    outgoing = jnp.take(coeff, source_rows.reshape(-1), axis=0)
    outgoing = jnp.where(filled.reshape(-1)[:, None, None], outgoing, jnp.zeros_like(outgoing))
    outgoing = outgoing.reshape(num_clusters, capacity, num_funcs, my_columns)
    incoming = lax.all_to_all(outgoing, "cluster", split_axis=0, concat_axis=0, tiled=True)
    my_owners = lax.dynamic_index_in_dim(owners, my_cluster, 0, keepdims=False)
    my_ranks = lax.dynamic_index_in_dim(slot_rank, my_cluster, 0, keepdims=False)
    positions = my_owners * capacity + my_ranks
    needed = jnp.take(
        incoming.reshape(num_clusters * capacity, num_funcs * my_columns), positions, axis=0
    )
    needed = needed.reshape(list_len * num_funcs, my_columns)
    local_vals = jnp.dot(
        basis_vals,
        lax.all_gather(needed, "blk", axis=1, tiled=True),
        preferred_element_type=jnp.float32,
    ).astype(jnp.bfloat16)
    norm_factor = local_vals.shape[1] ** (-0.5)
    my_reach = reach[0]

    def term(source, offset):
        return block_term(
            local_vals,
            source,
            coulomb[:, offset + half_stops, :],
            abs(offset) <= my_reach,
            norm_factor,
        )

    accumulated = term(local_vals, 0)
    upward = local_vals
    downward = local_vals
    for stop_num in range(1, half_stops + 1):
        upward = passed_along(upward, "blk", -1)
        accumulated = accumulated + term(upward, stop_num)
        downward = passed_along(downward, "blk", 1)
        accumulated = accumulated + term(downward, -stop_num)
    return accumulated.astype(jnp.bfloat16)


def solution(mesh):
    return jax.shard_map(
        on_device,
        mesh=mesh,
        in_specs=(
            P("cluster", None, "blk"),
            P(),
            P(("cluster", "blk"), None),
            P(("cluster", "blk"), None, None),
            P(("cluster", "blk")),
        ),
        out_specs=P(("cluster", "blk"), None),
        check_vma=False,
    )
```

profile of v0, /device:TPU:114, one launch (start us, length us, event | category | flops | bytes accessed | tf_op | source)
XLA Modules:
  0.0 255.3 jit_solution(13018517774100364596)
XLA Ops:
  6.5 0.0 copy-start
  6.5 0.8 broadcast_compare_fusion
  7.3 0.7 broadcast_subtract_fusion
  8.0 0.8 convert_reduce_fusion
  8.8 0.1 select_reduce_fusion
  8.9 0.1 copy.8
  9.0 0.1 fusion.70
  9.2 0.1 reshape.131
  9.3 0.1 copy.7
  9.4 0.1 copy.6
  9.5 1.5 gather_fusion
  11.0 0.9 select_select_fusion
  11.8 12.6 %all-to-all-start = ((bf16[32,2,8,128]{3,2,1,0:T(8,128)(2,1)}), bf16[32,2,8,128]{3,2,1,0:T(8,128)(2,1)S(1)}, u32[]{:S(2)}, u32[]{:S(2)}) async-start(bf16[32,2,8,128]{3,2,1,0:T(8,128)(2,1)} %select_select_fusion), calls=%async_computation | async-start | bytes 262144 | tf_op jit(solution)/shard_map/all_to_all | solution.py:49
  24.4 0.0 all-gather.2.cloned.1.call-start
  24.5 0.1 broadcast_in_dim.66
  24.5 0.1 broadcast_in_dim.67
  24.7 9.1 %all-to-all-done = bf16[32,2,8,128]{3,2,1,0:T(8,128)(2,1)S(1)} async-done(((bf16[32,2,8,128]{3,2,1,0:T(8,128)(2,1)}), bf16[32,2,8,128]{3,2,1,0:T(8,128)(2,1)S(1)}, u32[]{:S(2)}, u32[]{:S(2)}) %all-to-all-start) | async-done | bytes 131104 | tf_op jit(solution)/shard_map/all_to_all | solution.py:49
  33.8 0.6 gather_fusion.1
  34.4 0.7 broadcast_select_fusion
  35.2 0.0 all-gather.2.cloned.1.call-update
  35.2 77.8 %all-gather.2.cloned.1.call-done = bf16[256,2048]{1,0:T(8,128)(2,1)} async-done(((bf16[256,128]{1,0:T(8,128)(2,1)}), bf16[256,2048]{1,0:T(8,128)(2,1)}) %all-gather.2.cloned.1.call-update) | async-done | bytes 1048592 | tf_op jit(solution)/shard_map/all_gather | solution.py:59
  113.0 0.0 copy-done
  113.0 1.7 convolution_convert_fusion
  114.7 1.9 collective-permute-start.1
  116.6 3.9 %collective-permute-start = (bf16[256,2048]{0,1:T(8,128)(2,1)S(1)}, bf16[256,2048]{0,1:T(8,128)(2,1)}, u32[]{:S(2)}, u32[]{:S(2)}) collective-permute-start(bf16[256,2048]{0,1:T(8,128)(2,1)S(1)} %bitcast.85), channel_id=1, source_target_pairs={{0,15},{1,0},{2,1},{3,2},{4,3},{5,4},{6,5},{7,6},{8,7},{9,8},{10,9... | collective-permute-start | bytes 3145736 | tf_op jit(solution)/shard_map/ppermute | solution.py:10
  120.5 41.8 %collective-permute-done.1 = bf16[256,2048]{0,1:T(8,128)(2,1)} collective-permute-done((bf16[256,2048]{0,1:T(8,128)(2,1)S(1)}, bf16[256,2048]{0,1:T(8,128)(2,1)}, u32[]{:S(2)}, u32[]{:S(2)}) %collective-permute-start.1) | collective-permute-done | bytes 1048608 | tf_op jit(solution)/shard_map/ppermute | solution.py:10
  162.3 1.9 collective-permute-start.3
  164.9 0.0 collective-permute-done
  164.9 3.9 %collective-permute-start.2 = (bf16[256,2048]{0,1:T(8,128)(2,1)}, bf16[256,2048]{0,1:T(8,128)(2,1)}, u32[]{:S(2)}, u32[]{:S(2)}) collective-permute-start(bf16[256,2048]{0,1:T(8,128)(2,1)} %collective-permute-done), channel_id=1, source_target_pairs={{0,15},{1,0},{2,1},{3,2},{4,3},{5,4},{6,5},{7,6},{8,7},{9,8},{10,9... | collective-permute-start | bytes 3145736 | tf_op jit(solution)/shard_map/ppermute | solution.py:10
  168.9 2.2 fusion.26
  171.1 4.4 %convolution_add_fusion.3 = f32[256,2048]{1,0:T(8,128)} fusion(f32[256,2048]{1,0:T(8,128)S(1)} %fusion.26, bf16[256,2048]{0,1:T(8,128)(2,1)} %collective-permute-done, bf16[2048,256]{1,0:T(8,128)(2,1)S(1)} %convolution_convert_fusion, bf16[256,7,256]{2,0,1:T(8,128)(2,1)} %param.8, pred[]{:T(512)} %bitcast.7), kind=kOutput, calls=%fused_computation.7 | convolution fusion | flops 537722880 | bytes 7471616 | tf_op jit(solution)/shard_map/dot_general | solution.py:23
  175.4 35.8 %collective-permute-done.3 = bf16[256,2048]{0,1:T(8,128)(2,1)} collective-permute-done((bf16[256,2048]{0,1:T(8,128)(2,1)}, bf16[256,2048]{0,1:T(8,128)(2,1)}, u32[]{:S(2)}, u32[]{:S(2)}) %collective-permute-start.3) | collective-permute-done | bytes 1048608 | tf_op jit(solution)/shard_map/ppermute | solution.py:10
  211.2 1.9 collective-permute-start.5
  213.1 4.9 %convolution_add_fusion.2 = f32[256,2048]{1,0:T(8,128)} fusion(f32[256,2048]{1,0:T(8,128)} %convolution_add_fusion.3, bf16[256,2048]{0,1:T(8,128)(2,1)} %collective-permute-done.1, bf16[2048,256]{1,0:T(8,128)(2,1)S(1)} %convolution_convert_fusion, bf16[256,7,256]{2,0,1:T(8,128)(2,1)} %param.8, pred[]{:T(512)} %bitcast.7), kind=kOutput, calls=%fused_computation.6 | convolution fusion | flops 537722880 | bytes 7471616 | tf_op jit(solution)/shard_map/dot_general | solution.py:23
  218.1 0.0 collective-permute-done.2
  218.1 3.9 %collective-permute-start.4 = (bf16[256,2048]{0,1:T(8,128)(2,1)}, bf16[256,2048]{0,1:T(8,128)(2,1)}, u32[]{:S(2)}, u32[]{:S(2)}) collective-permute-start(bf16[256,2048]{0,1:T(8,128)(2,1)} %collective-permute-done.2), channel_id=1, source_target_pairs={{0,15},{1,0},{2,1},{3,2},{4,3},{5,4},{6,5},{7,6},{8,7},{9,8},{10,9... | collective-permute-start | bytes 3145736 | tf_op jit(solution)/shard_map/ppermute | solution.py:10
  222.0 2.9 %fusion.25 = f32[256,2048]{1,0:T(8,128)S(1)} fusion(bf16[256,2048]{0,1:T(8,128)(2,1)} %collective-permute-done.3, bf16[2048,256]{1,0:T(8,128)(2,1)S(1)} %convolution_convert_fusion, bf16[256,7,256]{2,0,1:T(8,128)(2,1)} %param.8, pred[]{:T(512)} %bitcast.11), kind=kOutput, calls=%fused_computation.39 | convolution fusion | flops 537198592 | bytes 5374464 | tf_op jit(solution)/shard_map/dot_general | solution.py:23
  224.9 4.9 %fusion.1 = f32[256,2048]{1,0:T(8,128)} fusion(f32[256,2048]{1,0:T(8,128)S(1)} %fusion.25, f32[256,2048]{1,0:T(8,128)} %convolution_add_fusion.2, bf16[256,2048]{0,1:T(8,128)(2,1)} %collective-permute-done.2, bf16[2048,256]{1,0:T(8,128)(2,1)S(1)} %convolution_convert_fusion, bf16[256,7,256]{2,0,1:T(8,128)(2,1)} %param.8, pred[]{:T(512)} %bitcast.11), kind=kOutput, calls=%fused_computation.5 | convolution fusion | flops 538247168 | bytes 9568768 | tf_op jit(solution)/shard_map/dot_general | solution.py:23
  229.8 9.6 %collective-permute-done.5 = bf16[256,2048]{0,1:T(8,128)(2,1)} collective-permute-done((bf16[256,2048]{0,1:T(8,128)(2,1)}, bf16[256,2048]{0,1:T(8,128)(2,1)}, u32[]{:S(2)}, u32[]{:S(2)}) %collective-permute-start.5) | collective-permute-done | bytes 1048608 | tf_op jit(solution)/shard_map/ppermute | solution.py:10
  239.4 0.0 copy-start.1
  239.4 4.4 %fusion.24 = f32[256,2048]{1,0:T(8,128)} fusion(bf16[256,2048]{0,1:T(8,128)(2,1)} %collective-permute-done.5, bf16[2048,256]{1,0:T(8,128)(2,1)S(1)} %convolution_convert_fusion, bf16[256,7,256]{2,0,1:T(8,128)(2,1)} %param.8, pred[]{:T(512)} %bitcast.14), kind=kOutput, calls=%fused_computation.38 | convolution fusion | flops 537198592 | bytes 5374464 | tf_op jit(solution)/shard_map/dot_general | solution.py:23
  243.8 0.0 collective-permute-done.4
  243.8 0.0 copy-done.1
  243.8 4.6 %fusion.2 = bf16[256,2048]{1,0:T(8,128)(2,1)} fusion(f32[256,2048]{1,0:T(8,128)} %fusion.24, f32[256,2048]{1,0:T(8,128)S(1)} %copy-done.1, bf16[256,2048]{0,1:T(8,128)(2,1)} %collective-permute-done.4, bf16[2048,256]{1,0:T(8,128)(2,1)S(1)} %convolution_convert_fusion, bf16[256,7,256]{2,0,1:T(8,128)(2,1)} %param.8, pred[]{:T(512)} %bitcast.14), kind=kOutput, calls=%fused_computation.8 | convolution fusion | flops 538771456 | bytes 8520192 | tf_op jit(solution)/shard_map/dot_general | solution.py:23
  (8 shorter events, 0.1 us)
Async XLA Ops:
  6.5 106.4 %copy-start = (bf16[256,256]{1,0:T(8,128)(2,1)S(1)}, bf16[256,256]{1,0:T(8,128)(2,1)}, u32[]{:S(2)}) copy-start(bf16[256,256]{1,0:T(8,128)(2,1)} %param.7) | copy-start | bytes 393220
  11.8 21.9 %all-to-all-start = ((bf16[32,2,8,128]{3,2,1,0:T(8,128)(2,1)}), bf16[32,2,8,128]{3,2,1,0:T(8,128)(2,1)S(1)}, u32[]{:S(2)}, u32[]{:S(2)}) async-start(bf16[32,2,8,128]{3,2,1,0:T(8,128)(2,1)} %select_select_fusion), calls=%async_computation | async-start | bytes 262144 | tf_op jit(solution)/shard_map/all_to_all | solution.py:49
  24.4 88.6 %all-gather.2.cloned.1.call-start = ((), (), s32[]{:S(2)}) async-start(), calls=%async_computation.1 | async-start | bytes 1114112 | tf_op jit(solution)/shard_map/all_gather | solution.py:59
  114.7 47.7 %collective-permute-start.1 = (bf16[256,2048]{0,1:T(8,128)(2,1)S(1)}, bf16[256,2048]{0,1:T(8,128)(2,1)}, u32[]{:S(2)}, u32[]{:S(2)}) collective-permute-start(bf16[256,2048]{0,1:T(8,128)(2,1)S(1)} %bitcast.84), channel_id=1, source_target_pairs={{0,1},{1,2},{2,3},{3,4},{4,5},{5,6},{6,7},{7,8},{8,9},{9,10},{10,1... | collective-permute-start | bytes 3145736 | tf_op jit(solution)/shard_map/ppermute | solution.py:10
  116.6 48.3 %collective-permute-start = (bf16[256,2048]{0,1:T(8,128)(2,1)S(1)}, bf16[256,2048]{0,1:T(8,128)(2,1)}, u32[]{:S(2)}, u32[]{:S(2)}) collective-permute-start(bf16[256,2048]{0,1:T(8,128)(2,1)S(1)} %bitcast.85), channel_id=1, source_target_pairs={{0,15},{1,0},{2,1},{3,2},{4,3},{5,4},{6,5},{7,6},{8,7},{9,8},{10,9... | collective-permute-start | bytes 3145736 | tf_op jit(solution)/shard_map/ppermute | solution.py:10
  162.3 48.9 %collective-permute-start.3 = (bf16[256,2048]{0,1:T(8,128)(2,1)}, bf16[256,2048]{0,1:T(8,128)(2,1)}, u32[]{:S(2)}, u32[]{:S(2)}) collective-permute-start(bf16[256,2048]{0,1:T(8,128)(2,1)} %collective-permute-done.1), channel_id=1, source_target_pairs={{0,1},{1,2},{2,3},{3,4},{4,5},{5,6},{6,7},{7,8},{8,9},{9,10},{10,1... | collective-permute-start | bytes 3145736 | tf_op jit(solution)/shard_map/ppermute | solution.py:10
  164.9 53.1 %collective-permute-start.2 = (bf16[256,2048]{0,1:T(8,128)(2,1)}, bf16[256,2048]{0,1:T(8,128)(2,1)}, u32[]{:S(2)}, u32[]{:S(2)}) collective-permute-start(bf16[256,2048]{0,1:T(8,128)(2,1)} %collective-permute-done), channel_id=1, source_target_pairs={{0,15},{1,0},{2,1},{3,2},{4,3},{5,4},{6,5},{7,6},{8,7},{9,8},{10,9... | collective-permute-start | bytes 3145736 | tf_op jit(solution)/shard_map/ppermute | solution.py:10
  211.2 28.2 %collective-permute-start.5 = (bf16[256,2048]{0,1:T(8,128)(2,1)}, bf16[256,2048]{0,1:T(8,128)(2,1)}, u32[]{:S(2)}, u32[]{:S(2)}) collective-permute-start(bf16[256,2048]{0,1:T(8,128)(2,1)} %collective-permute-done.3), channel_id=1, source_target_pairs={{0,1},{1,2},{2,3},{3,4},{4,5},{5,6},{6,7},{7,8},{8,9},{9,10},{10,1... | collective-permute-start | bytes 3145736 | tf_op jit(solution)/shard_map/ppermute | solution.py:10
  218.1 25.8 %collective-permute-start.4 = (bf16[256,2048]{0,1:T(8,128)(2,1)}, bf16[256,2048]{0,1:T(8,128)(2,1)}, u32[]{:S(2)}, u32[]{:S(2)}) collective-permute-start(bf16[256,2048]{0,1:T(8,128)(2,1)} %collective-permute-done.2), channel_id=1, source_target_pairs={{0,15},{1,0},{2,1},{3,2},{4,3},{5,4},{6,5},{7,6},{8,7},{9,8},{10,9... | collective-permute-start | bytes 3145736 | tf_op jit(solution)/shard_map/ppermute | solution.py:10
  239.4 4.4 %copy-start.1 = (f32[256,2048]{1,0:T(8,128)S(1)}, f32[256,2048]{1,0:T(8,128)}, u32[]{:S(2)}) copy-start(f32[256,2048]{1,0:T(8,128)} %fusion.1) | copy-start | bytes 6291460
Sparse Core Ops, SparseCore 0:
  35.3 77.6 all-gather.1
where the time goes:
time: 256 us; the launch traced here: 255 us
  waiting for transfers between devices  174 us (68%)
  starting transfers between devices  30.1 us (12%)
  matrix products  30.1 us (12%)
  between operations  14.2 us (6%)
  other arithmetic  4.15 us (2%)
  local copies, waits for them, and re-layouts  2.74 us (1%)
    ppermute x6, waiting for transfers between devices, passed_along(): return lax.ppermute(value, axis, pairs)  87.2 us
    all_gather x1, waiting for transfers between devices, on_device(): lax.all_gather(needed, 'blk', axis=1, tiled=True)  77.8 us
    dot_general x7, matrix products, block_term(): return jnp.dot(masked_tile, source, preferred_element_type=jnp.float32)  28.4 us
    ppermute x6, starting transfers between devices, passed_along(): return lax.ppermute(value, axis, pairs)  17.5 us
    all_to_all x1, starting transfers between devices, on_device(): lax.all_to_all(outgoing, 'cluster', split_axis=0, concat_axis=0, tiled=True)  12.6 us
    all_to_all x1, waiting for transfers between devices, on_device(): lax.all_to_all(outgoing, 'cluster', split_axis=0, concat_axis=0, tiled=True)  9.07 us
  transfers between devices with their start and end apart: 8, of which 5 were waited for; matrix products, arithmetic and copies ran while one was open for 9% of the time, Pallas kernels for 0%

commit v1 on v0

--- a/solution.py
+++ b/solution.py
@@ -56,7 +56,9 @@
     needed = needed.reshape(list_len * num_funcs, my_columns)
     local_vals = jnp.dot(
         basis_vals,
-        lax.all_gather(needed, "blk", axis=1, tiled=True),
+        jnp.concatenate(
+            lax.all_to_all(jnp.stack([needed] * lax.axis_size("blk")), "blk", 0, 0), axis=1
+        ),
         preferred_element_type=jnp.float32,
     ).astype(jnp.bfloat16)
     norm_factor = local_vals.shape[1] ** (-0.5)

time: 256 us -> 220 us (0.86)
  the two profiles are of different devices: /device:TPU:114 before, /device:TPU:1 now
where the time goes in v1:
time: 220 us; the launch traced here: 219 us
  waiting for transfers between devices  115 us (52%)
  blocking collectives  34.4 us (16%)
  starting transfers between devices  34.1 us (16%)
  matrix products  28.7 us (13%)
  other arithmetic  3.52 us (2%)
  local copies, waits for them, and re-layouts  2.94 us (1%)
    ppermute x6, waiting for transfers between devices, passed_along(): return lax.ppermute(value, axis, pairs)  104 us
    all_to_all x1, blocking collectives, on_device(): lax.all_to_all(jnp.stack([needed] * lax.axis_size('blk')), 'blk', 0, 0)  34.4 us
    dot_general x7, matrix products, block_term(): return jnp.dot(masked_tile, source, preferred_element_type=jnp.float32)  28.2 us
    ppermute x6, starting transfers between devices, passed_along(): return lax.ppermute(value, axis, pairs)  19.7 us
    all_to_all x1, starting transfers between devices, on_device(): lax.all_to_all(outgoing, 'cluster', split_axis=0, concat_axis=0, tiled=True)  14.4 us
    all_to_all x1, waiting for transfers between devices, on_device(): lax.all_to_all(outgoing, 'cluster', split_axis=0, concat_axis=0, tiled=True)  11.1 us
  transfers between devices with their start and end apart: 7, of which 6 were waited for; matrix products, arithmetic and copies ran while one was open for 11% of the time, Pallas kernels for 0%

profile of v1, /device:TPU:1, one launch (start us, length us, event | category | flops | bytes accessed | tf_op | source)
XLA Modules:
  0.0 219.4 jit_solution(9837043771213941112)
XLA Ops:
  0.0 0.0 copy-start
  0.0 0.8 broadcast_compare_fusion
  0.8 0.7 broadcast_subtract_fusion
  1.5 0.8 convert_reduce_fusion
  2.3 0.1 select_reduce_fusion
  2.4 0.1 copy.9
  2.5 0.1 fusion.70
  2.6 0.1 reshape.142
  2.8 0.1 copy.8
  2.9 0.1 copy.7
  3.0 1.5 gather_fusion
  4.4 0.9 select_select_fusion
  5.3 14.4 %all-to-all-start = ((bf16[32,2,8,128]{3,2,1,0:T(8,128)(2,1)}), bf16[32,2,8,128]{3,2,1,0:T(8,128)(2,1)S(1)}, u32[]{:S(2)}, u32[]{:S(2)}) async-start(bf16[32,2,8,128]{3,2,1,0:T(8,128)(2,1)} %select_select_fusion), calls=%async_computation | async-start | bytes 262144 | tf_op jit(solution)/shard_map/all_to_all | solution.py:49
  19.8 0.1 broadcast_in_dim.66
  19.8 0.1 broadcast_in_dim.67
  20.0 11.1 %all-to-all-done = bf16[32,2,8,128]{3,2,1,0:T(8,128)(2,1)S(1)} async-done(((bf16[32,2,8,128]{3,2,1,0:T(8,128)(2,1)}), bf16[32,2,8,128]{3,2,1,0:T(8,128)(2,1)S(1)}, u32[]{:S(2)}, u32[]{:S(2)}) %all-to-all-start) | async-done | bytes 131104 | tf_op jit(solution)/shard_map/all_to_all | solution.py:49
  31.1 0.6 gather_fusion.1
  31.8 0.1 broadcast_select_fusion
  31.9 0.1 copy.10
  32.0 0.1 stack.3
  32.1 34.4 %all_to_all.10 = bf16[16,256,128]{1,2,0:T(8,128)(2,1)S(1)} all-to-all(bf16[16,256,128]{1,2,0:T(8,128)(2,1)S(1)} %stack.3), channel_id=1, replica_groups=mesh['cluster'=32,'blk'=16] {'blk'}, dimensions={0} | all-to-all | bytes 2097152 | tf_op jit(solution)/shard_map/all_to_all | solution.py:60
  66.5 0.0 copy-done
  66.5 0.5 convolution_convert_fusion
  67.0 1.9 collective-permute-start.1
  68.9 5.5 %collective-permute-start = (bf16[256,2048]{0,1:T(8,128)(2,1)S(1)}, bf16[256,2048]{0,1:T(8,128)(2,1)}, u32[]{:S(2)}, u32[]{:S(2)}) collective-permute-start(bf16[256,2048]{0,1:T(8,128)(2,1)S(1)} %bitcast.88), channel_id=1, source_target_pairs={{0,15},{1,0},{2,1},{3,2},{4,3},{5,4},{6,5},{7,6},{8,7},{9,8},{10,9... | collective-permute-start | bytes 3145736 | tf_op jit(solution)/shard_map/ppermute | solution.py:10
  74.4 36.6 %collective-permute-done.1 = bf16[256,2048]{0,1:T(8,128)(2,1)} collective-permute-done((bf16[256,2048]{0,1:T(8,128)(2,1)S(1)}, bf16[256,2048]{0,1:T(8,128)(2,1)}, u32[]{:S(2)}, u32[]{:S(2)}) %collective-permute-start.1) | collective-permute-done | bytes 1048608 | tf_op jit(solution)/shard_map/ppermute | solution.py:10
  111.0 4.2 %collective-permute-start.3 = (bf16[256,2048]{0,1:T(8,128)(2,1)}, bf16[256,2048]{0,1:T(8,128)(2,1)}, u32[]{:S(2)}, u32[]{:S(2)}) collective-permute-start(bf16[256,2048]{0,1:T(8,128)(2,1)} %collective-permute-done.1), channel_id=1, source_target_pairs={{0,1},{1,2},{2,3},{3,4},{4,5},{5,6},{6,7},{7,8},{8,9},{9,10},{10,1... | collective-permute-start | bytes 3145736 | tf_op jit(solution)/shard_map/ppermute | solution.py:10
  115.8 24.9 %collective-permute-done = bf16[256,2048]{0,1:T(8,128)(2,1)} collective-permute-done((bf16[256,2048]{0,1:T(8,128)(2,1)S(1)}, bf16[256,2048]{0,1:T(8,128)(2,1)}, u32[]{:S(2)}, u32[]{:S(2)}) %collective-permute-start) | collective-permute-done | bytes 1048608 | tf_op jit(solution)/shard_map/ppermute | solution.py:10
  140.8 1.9 collective-permute-start.2
  142.7 2.2 %fusion.26 = f32[256,2048]{1,0:T(8,128)S(1)} fusion(bf16[2048,256]{1,0:T(8,128)(2,1)S(1)} %convolution_convert_fusion, bf16[256,7,256]{2,0,1:T(8,128)(2,1)} %param.8, pred[]{:T(512)} %bitcast), kind=kOutput, calls=%fused_computation.40 | convolution fusion | flops 537198592 | bytes 5374464 | tf_op jit(solution)/shard_map/dot_general | solution.py:23
  144.9 4.3 %convolution_add_fusion.3 = f32[256,2048]{1,0:T(8,128)} fusion(f32[256,2048]{1,0:T(8,128)S(1)} %fusion.26, bf16[256,2048]{0,1:T(8,128)(2,1)} %collective-permute-done, bf16[2048,256]{1,0:T(8,128)(2,1)S(1)} %convolution_convert_fusion, bf16[256,7,256]{2,0,1:T(8,128)(2,1)} %param.8, pred[]{:T(512)} %bitcast.9), kind=kOutput, calls=%fused_computation.7 | convolution fusion | flops 537722880 | bytes 7471616 | tf_op jit(solution)/shard_map/dot_general | solution.py:23
  149.2 7.3 %collective-permute-done.3 = bf16[256,2048]{0,1:T(8,128)(2,1)} collective-permute-done((bf16[256,2048]{0,1:T(8,128)(2,1)}, bf16[256,2048]{0,1:T(8,128)(2,1)}, u32[]{:S(2)}, u32[]{:S(2)}) %collective-permute-start.3) | collective-permute-done | bytes 1048608 | tf_op jit(solution)/shard_map/ppermute | solution.py:10
  156.5 4.2 %collective-permute-start.5 = (bf16[256,2048]{0,1:T(8,128)(2,1)}, bf16[256,2048]{0,1:T(8,128)(2,1)}, u32[]{:S(2)}, u32[]{:S(2)}) collective-permute-start(bf16[256,2048]{0,1:T(8,128)(2,1)} %collective-permute-done.3), channel_id=1, source_target_pairs={{0,1},{1,2},{2,3},{3,4},{4,5},{5,6},{6,7},{7,8},{8,9},{9,10},{10,1... | collective-permute-start | bytes 3145736 | tf_op jit(solution)/shard_map/ppermute | solution.py:10
  160.7 4.9 %convolution_add_fusion.2 = f32[256,2048]{1,0:T(8,128)} fusion(f32[256,2048]{1,0:T(8,128)} %convolution_add_fusion.3, bf16[256,2048]{0,1:T(8,128)(2,1)} %collective-permute-done.1, bf16[2048,256]{1,0:T(8,128)(2,1)S(1)} %convolution_convert_fusion, bf16[256,7,256]{2,0,1:T(8,128)(2,1)} %param.8, pred[]{:T(512)} %bitcast.9), kind=kOutput, calls=%fused_computation.6 | convolution fusion | flops 537722880 | bytes 7471616 | tf_op jit(solution)/shard_map/dot_general | solution.py:23
  165.6 23.8 %collective-permute-done.2 = bf16[256,2048]{0,1:T(8,128)(2,1)} collective-permute-done((bf16[256,2048]{0,1:T(8,128)(2,1)}, bf16[256,2048]{0,1:T(8,128)(2,1)}, u32[]{:S(2)}, u32[]{:S(2)}) %collective-permute-start.2) | collective-permute-done | bytes 1048608 | tf_op jit(solution)/shard_map/ppermute | solution.py:10
  189.5 1.9 collective-permute-start.4
  191.4 2.9 %fusion.25 = f32[256,2048]{1,0:T(8,128)S(1)} fusion(bf16[256,2048]{0,1:T(8,128)(2,1)} %collective-permute-done.3, bf16[2048,256]{1,0:T(8,128)(2,1)S(1)} %convolution_convert_fusion, bf16[256,7,256]{2,0,1:T(8,128)(2,1)} %param.8, pred[]{:T(512)} %bitcast.13), kind=kOutput, calls=%fused_computation.39 | convolution fusion | flops 537198592 | bytes 5374464 | tf_op jit(solution)/shard_map/dot_general | solution.py:23
  194.3 4.9 %fusion.1 = f32[256,2048]{1,0:T(8,128)} fusion(f32[256,2048]{1,0:T(8,128)S(1)} %fusion.25, f32[256,2048]{1,0:T(8,128)} %convolution_add_fusion.2, bf16[256,2048]{0,1:T(8,128)(2,1)} %collective-permute-done.2, bf16[2048,256]{1,0:T(8,128)(2,1)S(1)} %convolution_convert_fusion, bf16[256,7,256]{2,0,1:T(8,128)(2,1)} %param.8, pred[]{:T(512)} %bitcast.13), kind=kOutput, calls=%fused_computation.5 | convolution fusion | flops 538247168 | bytes 9568768 | tf_op jit(solution)/shard_map/dot_general | solution.py:23
  199.2 0.0 collective-permute-done.5
  199.2 0.0 copy-start.1
  199.2 4.4 %fusion.24 = f32[256,2048]{1,0:T(8,128)} fusion(bf16[256,2048]{0,1:T(8,128)(2,1)} %collective-permute-done.5, bf16[2048,256]{1,0:T(8,128)(2,1)S(1)} %convolution_convert_fusion, bf16[256,7,256]{2,0,1:T(8,128)(2,1)} %param.8, pred[]{:T(512)} %bitcast.16), kind=kOutput, calls=%fused_computation.38 | convolution fusion | flops 537198592 | bytes 5374464 | tf_op jit(solution)/shard_map/dot_general | solution.py:23
  203.6 11.2 %collective-permute-done.4 = bf16[256,2048]{0,1:T(8,128)(2,1)} collective-permute-done((bf16[256,2048]{0,1:T(8,128)(2,1)}, bf16[256,2048]{0,1:T(8,128)(2,1)}, u32[]{:S(2)}, u32[]{:S(2)}) %collective-permute-start.4) | collective-permute-done | bytes 1048608 | tf_op jit(solution)/shard_map/ppermute | solution.py:10
  214.8 0.0 copy-done.1
  214.8 4.6 %fusion.2 = bf16[256,2048]{1,0:T(8,128)(2,1)} fusion(f32[256,2048]{1,0:T(8,128)} %fusion.24, f32[256,2048]{1,0:T(8,128)S(1)} %copy-done.1, bf16[256,2048]{0,1:T(8,128)(2,1)} %collective-permute-done.4, bf16[2048,256]{1,0:T(8,128)(2,1)S(1)} %convolution_convert_fusion, bf16[256,7,256]{2,0,1:T(8,128)(2,1)} %param.8, pred[]{:T(512)} %bitcast.16), kind=kOutput, calls=%fused_computation.8 | convolution fusion | flops 538771456 | bytes 8520192 | tf_op jit(solution)/shard_map/dot_general | solution.py:23
  (8 shorter events, 0.1 us)
Async XLA Ops:
  0.0 66.5 %copy-start = (bf16[256,256]{1,0:T(8,128)(2,1)S(1)}, bf16[256,256]{1,0:T(8,128)(2,1)}, u32[]{:S(2)}) copy-start(bf16[256,256]{1,0:T(8,128)(2,1)} %param.7) | copy-start | bytes 393220
  5.3 25.8 %all-to-all-start = ((bf16[32,2,8,128]{3,2,1,0:T(8,128)(2,1)}), bf16[32,2,8,128]{3,2,1,0:T(8,128)(2,1)S(1)}, u32[]{:S(2)}, u32[]{:S(2)}) async-start(bf16[32,2,8,128]{3,2,1,0:T(8,128)(2,1)} %select_select_fusion), calls=%async_computation | async-start | bytes 262144 | tf_op jit(solution)/shard_map/all_to_all | solution.py:49
  67.0 44.0 %collective-permute-start.1 = (bf16[256,2048]{0,1:T(8,128)(2,1)S(1)}, bf16[256,2048]{0,1:T(8,128)(2,1)}, u32[]{:S(2)}, u32[]{:S(2)}) collective-permute-start(bf16[256,2048]{0,1:T(8,128)(2,1)S(1)} %bitcast.87), channel_id=1, source_target_pairs={{0,1},{1,2},{2,3},{3,4},{4,5},{5,6},{6,7},{7,8},{8,9},{9,10},{10,1... | collective-permute-start | bytes 3145736 | tf_op jit(solution)/shard_map/ppermute | solution.py:10
  68.9 71.8 %collective-permute-start = (bf16[256,2048]{0,1:T(8,128)(2,1)S(1)}, bf16[256,2048]{0,1:T(8,128)(2,1)}, u32[]{:S(2)}, u32[]{:S(2)}) collective-permute-start(bf16[256,2048]{0,1:T(8,128)(2,1)S(1)} %bitcast.88), channel_id=1, source_target_pairs={{0,15},{1,0},{2,1},{3,2},{4,3},{5,4},{6,5},{7,6},{8,7},{9,8},{10,9... | collective-permute-start | bytes 3145736 | tf_op jit(solution)/shard_map/ppermute | solution.py:10
  111.0 45.5 %collective-permute-start.3 = (bf16[256,2048]{0,1:T(8,128)(2,1)}, bf16[256,2048]{0,1:T(8,128)(2,1)}, u32[]{:S(2)}, u32[]{:S(2)}) collective-permute-start(bf16[256,2048]{0,1:T(8,128)(2,1)} %collective-permute-done.1), channel_id=1, source_target_pairs={{0,1},{1,2},{2,3},{3,4},{4,5},{5,6},{6,7},{7,8},{8,9},{9,10},{10,1... | collective-permute-start | bytes 3145736 | tf_op jit(solution)/shard_map/ppermute | solution.py:10
  140.8 48.7 %collective-permute-start.2 = (bf16[256,2048]{0,1:T(8,128)(2,1)}, bf16[256,2048]{0,1:T(8,128)(2,1)}, u32[]{:S(2)}, u32[]{:S(2)}) collective-permute-start(bf16[256,2048]{0,1:T(8,128)(2,1)} %collective-permute-done), channel_id=1, source_target_pairs={{0,15},{1,0},{2,1},{3,2},{4,3},{5,4},{6,5},{7,6},{8,7},{9,8},{10,9... | collective-permute-start | bytes 3145736 | tf_op jit(solution)/shard_map/ppermute | solution.py:10
  156.5 42.8 %collective-permute-start.5 = (bf16[256,2048]{0,1:T(8,128)(2,1)}, bf16[256,2048]{0,1:T(8,128)(2,1)}, u32[]{:S(2)}, u32[]{:S(2)}) collective-permute-start(bf16[256,2048]{0,1:T(8,128)(2,1)} %collective-permute-done.3), channel_id=1, source_target_pairs={{0,1},{1,2},{2,3},{3,4},{4,5},{5,6},{6,7},{7,8},{8,9},{9,10},{10,1... | collective-permute-start | bytes 3145736 | tf_op jit(solution)/shard_map/ppermute | solution.py:10
  189.5 25.3 %collective-permute-start.4 = (bf16[256,2048]{0,1:T(8,128)(2,1)}, bf16[256,2048]{0,1:T(8,128)(2,1)}, u32[]{:S(2)}, u32[]{:S(2)}) collective-permute-start(bf16[256,2048]{0,1:T(8,128)(2,1)} %collective-permute-done.2), channel_id=1, source_target_pairs={{0,15},{1,0},{2,1},{3,2},{4,3},{5,4},{6,5},{7,6},{8,7},{9,8},{10,9... | collective-permute-start | bytes 3145736 | tf_op jit(solution)/shard_map/ppermute | solution.py:10
  199.2 15.5 %copy-start.1 = (f32[256,2048]{1,0:T(8,128)S(1)}, f32[256,2048]{1,0:T(8,128)}, u32[]{:S(2)}) copy-start(f32[256,2048]{1,0:T(8,128)} %fusion.1) | copy-start | bytes 6291460
